TPU v7x, 32 devices: a whole 2x2x4 slice. The times are simulated.
32 devices in a mesh: groups: 2 (over x), wide: 16 (over z, y, core).
Axes of the slice: x: 2, y: 2, z: 4, core: 2. Of those that a mesh axis runs over, the one named last changes fastest.
Arguments:
- tokens: bfloat16 [128, 16384], P('groups', 'wide'), parts along dimension 0, may hold values from -1.5 to 1.5
- norm_gain: bfloat16 [16384], P('wide'), may hold values from 0.099609375 to 1.8984375
- w_query: bfloat16 [16384, 8192], P('wide'), may hold values from -0.046875 to 0.046875
- key_weight: bfloat16 [16384, 512], P('wide'), may hold values from -0.046875 to 0.046875
- value_weight: bfloat16 [16384, 512], P('wide'), may hold values from -0.046875 to 0.046875
- w_out: bfloat16 [8192, 16384], P(None, 'wide'), may hold values from -0.0625 to 0.0625
- cache_keys: bfloat16 [128, 1024, 512], P(('groups', 'wide')), parts along dimension 0, may hold values from -1210 to 1210
- value_cache_slots: bfloat16 [128, 1024, 512], P(('groups', 'wide')), parts along dimension 0, may hold values from -6 to 6
- slot_fill_lengths: int32 [128], P(('groups', 'wide')), parts along dimension 0, may hold values from 1 to 1023, as said below
- slot_rows: int32 [128], P('groups'), parts along dimension 0, may hold values from 0 to 63, each once
Outputs:
- mixed: bfloat16 [128, 16384], P('groups', 'wide'), parts along dimension 0
- new_entries: bfloat16 [2, 128, 512], P(None, ('groups', 'wide')), parts along dimension 1
There are 2 independent parts, one for each index of `groups`. A program takes and returns all parts, laid end to end along the dimension named above; an argument that names none is the same for every part. Nothing has to cross between parts.
Inputs may be any that keep to these rules, and one draw needn't show every extreme that they name: `slot_fill_lengths`: every slot has at least one filled position and room for the new token; some slot is filled to 1023 and some to 1.
All inputs are finite; a program needn't handle non-finite values.
Results may differ from a plain program's by a relative error of at most 0.012.
The roundings to bfloat16 on the way count: a program that leaves them out, or rounds other values in their place, can miss the bound.
Values may be sent and summed in bfloat16 or wider, within the bound.
A program may use at most 128 MiB of HBM per device.

v0:
```python
import jax
import jax.numpy as jnp
from jax import lax
from jax.sharding import PartitionSpec as P

MODEL_WIDTH = 16384
HEAD_SIZE = 128
QUERY_HEADS = 64
KEY_VALUE_HEADS = 4


def apply_rotary(slot_values, positions, heads):
    filled_count = slot_values.shape[0]
    half = HEAD_SIZE // 2
    freq = 500000.0 ** (-(2.0 / HEAD_SIZE) * jnp.arange(half, dtype=jnp.float32))
    angle = positions.astype(jnp.float32)[:, None] * freq[None, :]
    cosine = jnp.cos(angle)[:, None, :]
    sine = jnp.sin(angle)[:, None, :]
    shaped = slot_values.reshape(filled_count, heads, HEAD_SIZE)
    first = shaped[..., :half]
    second = shaped[..., half:]
    joined = jnp.concatenate(
        [first * cosine - second * sine, second * cosine + first * sine], axis=2
    )
    return joined.reshape(filled_count, heads * HEAD_SIZE)


def attend(query_vector, fresh_key, fresh_value, slot_keys, slot_values, lengths):
    filled_count = query_vector.shape[0]
    query_group = QUERY_HEADS // KEY_VALUE_HEADS
    slot_room = slot_keys.shape[1]
    query_by_head = query_vector.reshape(filled_count, KEY_VALUE_HEADS, query_group, HEAD_SIZE)
    keys_by_head = slot_keys.reshape(filled_count, slot_room, KEY_VALUE_HEADS, HEAD_SIZE)
    values_by_head = slot_values.reshape(filled_count, slot_room, KEY_VALUE_HEADS, HEAD_SIZE)
    scale_factor = HEAD_SIZE ** (-0.5)
    scores = (
        jnp.einsum(
            "rkgd,rpkd->rkgp", query_by_head, keys_by_head, preferred_element_type=jnp.float32
        )
        * scale_factor
    )
    live = jnp.arange(slot_room, dtype=jnp.int32)[None, :] < lengths[:, None]
    scores = jnp.where(live[:, None, None, :], scores, -1e30)
    local_share = (
        jnp.einsum(
            "rkgd,rkd->rkg",
            query_by_head,
            fresh_key.reshape(filled_count, KEY_VALUE_HEADS, HEAD_SIZE),
            preferred_element_type=jnp.float32,
        )
        * scale_factor
    )
    top = jnp.maximum(jnp.max(scores, axis=3), local_share)
    weights = jnp.exp(scores - top[..., None])
    own_weight = jnp.exp(local_share - top)
    total = jnp.sum(weights, axis=3) + own_weight
    rounded = weights.astype(jnp.bfloat16)
    local_share_rounded = own_weight.astype(jnp.bfloat16).astype(jnp.float32)
    reduced_sum = jnp.einsum(
        "rkgp,rpkd->rkgd", rounded, values_by_head, preferred_element_type=jnp.float32
    )
    reduced_sum = reduced_sum + local_share_rounded[..., None] * fresh_value.reshape(
        filled_count, KEY_VALUE_HEADS, 1, HEAD_SIZE
    ).astype(jnp.float32)
    return (
        (reduced_sum / total[..., None])
        .reshape(filled_count, QUERY_HEADS * HEAD_SIZE)
        .astype(jnp.bfloat16)
    )


def body(
    tokens,
    norm_gain,
    w_query,
    key_weight,
    value_weight,
    w_out,
    cache_keys,
    value_cache_slots,
    slot_fill_lengths,
    slot_rows,
):
    local = cache_keys.shape[0]
    index = lax.axis_index("wide")
    ordered = tokens[slot_rows]
    ordered_f = ordered.astype(jnp.float32)
    squares = jnp.sum(ordered_f * ordered_f, axis=1)
    gained = (ordered_f * norm_gain.astype(jnp.float32)[None, :]).astype(jnp.bfloat16)
    every_term, every_square = lax.psum(
        (
            jnp.concatenate(
                [
                    jnp.dot(gained, w_query, preferred_element_type=jnp.float32),
                    jnp.dot(gained, key_weight, preferred_element_type=jnp.float32),
                    jnp.dot(gained, value_weight, preferred_element_type=jnp.float32),
                ],
                axis=1,
            ),
            squares,
        ),
        "wide",
    )
    reduced_sum = lax.dynamic_slice_in_dim(every_term, index * local, local, 0)
    mine = lax.dynamic_slice_in_dim(every_square, index * local, local, 0)
    score_scale = lax.rsqrt(mine / MODEL_WIDTH + 1e-05)[:, None]
    raw_q = reduced_sum[:, : QUERY_HEADS * HEAD_SIZE] * score_scale
    unrotated_key = (
        reduced_sum[:, QUERY_HEADS * HEAD_SIZE : (QUERY_HEADS + KEY_VALUE_HEADS) * HEAD_SIZE]
        * score_scale
    )
    projected_value = reduced_sum[:, (QUERY_HEADS + KEY_VALUE_HEADS) * HEAD_SIZE :] * score_scale
    query_vector = apply_rotary(raw_q, slot_fill_lengths, QUERY_HEADS).astype(jnp.bfloat16)
    fresh_key = apply_rotary(unrotated_key, slot_fill_lengths, KEY_VALUE_HEADS).astype(jnp.bfloat16)
    fresh_value = projected_value.astype(jnp.bfloat16)
    heads = attend(
        query_vector, fresh_key, fresh_value, cache_keys, value_cache_slots, slot_fill_lengths
    )
    projected = jnp.dot(
        lax.all_gather(heads, "wide", axis=0, tiled=True), w_out, preferred_element_type=jnp.float32
    )
    filled_count = slot_rows.shape[0]
    inverse = (
        jnp.zeros((filled_count,), jnp.int32)
        .at[slot_rows]
        .set(jnp.arange(filled_count, dtype=jnp.int32))
    )
    mixed = (tokens.astype(jnp.float32) + projected[inverse]).astype(jnp.bfloat16)
    return (mixed, jnp.stack([fresh_key, fresh_value]))


def solution(mesh):
    placed = (
        P("groups", "wide"),
        P("wide"),
        P("wide", None),
        P("wide", None),
        P("wide", None),
        P(None, "wide"),
        P(("groups", "wide"), None, None),
        P(("groups", "wide"), None, None),
        P(("groups", "wide")),
        P("groups"),
    )
    return jax.shard_map(
        body,
        mesh=mesh,
        in_specs=placed,
        out_specs=(P("groups", "wide"), P(None, ("groups", "wide"), None)),
        check_vma=False,
    )
```

profile of v0, /device:TPU:0, one launch (start us, length us, event | category | flops | bytes accessed | tf_op | source)
XLA Modules:
  0.0 188.2 jit_solution(17373420408250450581)
XLA Ops:
  7.2 0.7 compare_select_fusion.1
  8.0 0.7 convert_element_type.69
  8.7 1.7 gather_fusion
  10.4 0.3 fusion.30
  10.7 1.5 fusion.28
  12.2 8.8 %fusion.32 = f32[64,8192]{1,0:T(8,128)S(1)} fusion(bf16[1024,8192]{1,0:T(8,128)(2,1)} %param.12, bf16[64,1024]{1,0:T(8,128)(2,1)S(1)} %gather_fusion, f32[1024]{0:T(1024)S(1)} %convert_element_type.69), kind=kOutput, calls=%fused_computation.31 | convolution fusion | flops 1073938432 | bytes 19009536 | tf_op jit(solution)/shard_map/dot_general | solution.py:94
  21.0 1.5 pad_maximum_fusion
  22.6 0.1 fusion.26
  22.8 35.2 %psum.15 = f32[64]{0:T(128)S(1)} all-reduce(f32[64]{0:T(128)S(1)} %fusion.26), channel_id=1, replica_groups=mesh['groups'=2,'wide'=16] {'wide'}, use_global_device_ids=true, to_apply=%region_2.0 | all-reduce | flops 64 | bytes 512 | tf_op jit(solution)/shard_map/psum | solution.py:90
  58.0 0.1 add_rsqrt_fusion
  58.1 0.1 iota_compare_fusion
  58.2 0.1 multiply_cosine_fusion
  58.3 66.5 %all-reduce.2.cloned.1.call-done = f32[64,9216]{1,0:T(8,128)} async-done(((f32[64,9216]{1,0:T(8,128)}), f32[64,9216]{1,0:T(8,128)}) %all-reduce.2.cloned.1.call-update) | async-done | bytes 2359312 | tf_op jit(solution)/shard_map/psum | solution.py:90
  124.7 0.8 fusion.34
  125.6 1.0 fusion.27
  126.6 0.1 subtract_convert_fusion
  126.8 0.1 multiply_subtract_fusion
  126.9 0.1 pad_maximum_fusion.1
  126.9 0.1 fusion.49
  127.0 0.1 fusion.35
  127.2 3.7 %fusion.40 = (f32[4,4,16]{2,1,0:T(4,128)S(1)}, f32[4,4,16,1024]{3,2,1,0:T(8,128)S(1)}) fusion(bf16[4,4,16,128]{3,2,1,0:T(8,128)(2,1)S(1)} %bitcast.49, pred[4,1024]{1,0:T(4,128)(4,1)S(1)} %iota_compare_fusion, bf16[4,1024,512]{2,1,0:T(8,128)(2,1)} %param.16), kind=kOutput, calls=%fused_computation.57 | convolution fusion | flops 67895040 | bytes 5313536 | tf_op jit(solution)/shard_map/rkgd,rpkd->rkgp/dot_general | solution.py:37
  130.8 0.3 fusion.21
  131.2 0.7 fusion.18
  131.9 0.7 reshape.149
  132.6 0.8 scatter_custom_fusion
  133.4 0.1 maximum_convert_fusion
  133.5 0.6 pad_maximum_fusion.2
  134.2 35.6 %all-gather.3.cloned.1.call-done = bf16[16,4,8192]{2,1,0:T(4,128)(2,1)} async-done(((bf16[1,4,8192]{2,1,0:T(4,128)(2,1)}), bf16[16,4,8192]{2,1,0:T(4,128)(2,1)}) %all-gather.3.cloned.1.call-update) | async-done | bytes 1048592 | tf_op jit(solution)/shard_map/all_gather | solution.py:120
  169.8 1.3 reshape.150
  171.1 8.8 %fusion.41 = f32[64,1024]{1,0:T(8,128)S(1)} fusion(bf16[64,8192]{1,0:T(8,128)(2,1)S(1)} %reshape.150, bf16[8192,1024]{1,0:T(8,128)(2,1)} %param.15), kind=kOutput, calls=%fused_computation.58 | convolution fusion | flops 1073741824 | bytes 18087936 | tf_op jit(solution)/shard_map/dot_general | solution.py:119
  179.9 0.7 gather_fusion.1
  180.6 0.7 add_convert_fusion
  (24 shorter events, 0.2 us)
Async XLA Ops:
  7.2 3.2 %copy-start = (bf16[1024,512]{1,0:T(8,128)(2,1)S(1)}, bf16[1024,512]{1,0:T(8,128)(2,1)}, u32[]{:S(2)}) copy-start(bf16[1024,512]{1,0:T(8,128)(2,1)} %param.13) | copy-start | bytes 3145732
  7.2 117.6 %all-reduce.2.cloned.1.call-start = ((), (), s32[]{:S(2)}) async-start(), calls=%async_computation | async-start | bytes 4718592 | tf_op jit(solution)/shard_map/psum | solution.py:90
  21.0 1.6 copy-start.2
  22.6 147.2 %all-gather.3.cloned.1.call-start = ((), (), s32[]{:S(2)}) async-start(), calls=%async_computation.1 | async-start | bytes 1114112 | tf_op jit(solution)/shard_map/all_gather | solution.py:120
  126.8 4.3 %copy-start.3 = (bf16[4,1024,512]{2,1,0:T(8,128)(2,1)S(1)}, bf16[4,1024,512]{2,1,0:T(8,128)(2,1)}, u32[]{:S(2)}) copy-start(bf16[4,1024,512]{2,1,0:T(8,128)(2,1)} %param.17) | copy-start | bytes 12582916
  171.1 9.5 %copy-start.1 = (bf16[64,1024]{1,0:T(8,128)(2,1)S(1)}, bf16[64,1024]{1,0:T(8,128)(2,1)}, u32[]{:S(2)}) copy-start(bf16[64,1024]{1,0:T(8,128)(2,1)} %param.10) | copy-start | bytes 393220
Sparse Core Ops, SparseCore 0:
  22.7 102.0 all-reduce.1
  132.7 36.9 all-gather.2
where the time goes:
time: 189 us; the launch traced here: 188 us
  waiting for transfers between devices  102 us (54%)
  blocking collectives  35.2 us (19%)
  matrix products  23.9 us (13%)
  between operations  14.2 us (8%)
  other arithmetic  7.3 us (4%)
  local copies, waits for them, and re-layouts  5.26 us (3%)
    psum x1, waiting for transfers between devices, body(): lax.psum((jnp.concatenate([jnp.dot(gained, w_query, preferred_element_typ...  66.5 us
    all_gather x1, waiting for transfers between devices, body(): lax.all_gather(heads, 'wide', axis=0, tiled=True)  35.6 us
    psum x1, blocking collectives, body(): lax.psum((jnp.concatenate([jnp.dot(gained, w_query, preferred_element_typ...  35.2 us
    dot_general x1, matrix products, body(): jnp.dot(lax.all_gather(heads, 'wide', axis=0, tiled=True), w_out, preferr...  8.82 us
    dot_general x1, matrix products, body(): jnp.dot(gained, w_query, preferred_element_type=jnp.float32)  8.79 us
  transfers between devices with their start and end apart: 2, of which 2 were waited for; matrix products, arithmetic and copies ran while one was open for 1% of the time, Pallas kernels for 0%

commit v1 on v0

v1 whole, which is shorter than its diff:
```python
import functools

import jax
import jax.numpy as jnp
import numpy as np
from jax import lax
from jax.experimental import pallas as pl
from jax.experimental.pallas import tpu as pltpu
from jax.sharding import PartitionSpec as P

HEAD = 128
KV_HEADS = 4
GROUP = 16
QCOLS = GROUP * HEAD
KVCOLS = KV_HEADS * HEAD
SIDE = 2 * KVCOLS + HEAD
F32 = jnp.float32
BF16 = jnp.bfloat16
NT = (((1,), (1,)), ((), ()))


def iota(shape, axis):
    return lax.broadcasted_iota(jnp.int32, shape, axis)


def one_hot(condition):
    return jnp.where(condition, 1.0, 0.0).astype(BF16)


def reversed_bits(value, bits):
    out = jnp.zeros_like(value)
    for b in range(bits):
        out = out + ((value >> b) & 1) * (1 << (bits - 1 - b))
    return out


def dot(a, b):
    return jnp.dot(a, b, preferred_element_type=F32)


def kernel(n, stages, local, room, width,
           lengths, tokens, gain, rows_of, freq, wq_hbm, wk_hbm, wv_hbm, wo_hbm, kc_hbm, vc_hbm,
           mixed, entries,
           wq, wk, wv, wo, kc, vc, gained, side, queries, *rest):
    side_in = rest[:stages]
    query_in = rest[stages:2 * stages]
    (side_out, query_out, gathered, qs, hs, cos_tile, sin_tile, fresh, picks, total_out,
     w_sem, rs_send, rs_recv, ag_send, ag_recv) = rest[2 * stages:]
    rows = n * local
    parts = 16 // local
    per = GROUP // parts
    block = 16
    me = lax.axis_index("wide")
    bits = [(me // (1 << b)) % 2 for b in range(stages)]
    partner = [me + (1 - 2 * bits[b]) * (1 << b) for b in range(stages)]
    base = [jnp.int32(0)]
    for b in range(stages):
        base.append(base[-1] + bits[b] * (n >> (b + 1)))

    def weight_copy(i):
        if i == 0:
            return [pltpu.make_async_copy(wk_hbm, wk, w_sem.at[0]),
                    pltpu.make_async_copy(wv_hbm, wv, w_sem.at[1])]
        if i <= KV_HEADS:
            g = i - 1
            return [pltpu.make_async_copy(wq_hbm.at[:, pl.ds(g * QCOLS, QCOLS)], wq.at[g], w_sem.at[2 + g])]
        if i == KV_HEADS + 1:
            return [pltpu.make_async_copy(kc_hbm, kc, w_sem.at[6]),
                    pltpu.make_async_copy(vc_hbm, vc, w_sem.at[7])]
        g = i - KV_HEADS - 2
        return [pltpu.make_async_copy(wo_hbm.at[pl.ds(g * QCOLS, QCOLS)], wo.at[pl.ds(g * QCOLS, QCOLS)],
                                      w_sem.at[8 + g])]

    def begin(i):
        for c in weight_copy(i):
            c.start()

    def arrived(i):
        for c in weight_copy(i):
            c.wait()

    for i in range(KV_HEADS + 1):
        begin(i)

    barrier = pltpu.get_barrier_semaphore()
    for b in range(stages):
        pl.semaphore_signal(barrier, inc=1, device_id={"wide": partner[b]},
                            device_id_type=pl.DeviceIdType.MESH)

    slot_rows = rows_of[...]
    place = iota((rows, rows), 0)
    slot_at = reversed_bits(place // local, stages) * local + place % local
    reorder = one_hot(slot_at == iota((rows, rows), 1))
    row_of_slot = one_hot(iota((rows, rows), 0) == slot_rows)
    pick_tokens = lax.dot_general(reorder, row_of_slot, NT, preferred_element_type=F32).astype(BF16)
    ordered = dot(pick_tokens, tokens[...])
    gained[...] = (ordered * gain[...].astype(F32)).astype(BF16)
    squares = jnp.sum(ordered * ordered, axis=1, keepdims=True)
    side[:, 2 * KVCOLS:] = jnp.broadcast_to(squares, (rows, HEAD))

    wide_rows = parts * rows
    j = iota((rows, wide_rows), 1)
    slot_j = reversed_bits(j // block, stages) * local + j % local
    spread = one_hot(slot_j == iota((rows, wide_rows), 0))
    rows_bf = jnp.broadcast_to(slot_rows, (8, rows)).astype(F32).astype(BF16)
    row_j = dot(rows_bf, spread)[:1].astype(jnp.int32)
    out_row = iota((wide_rows, 1), 0)
    part_j = (iota((1, wide_rows), 1) % block) // local
    picks[...] = one_hot(jnp.logical_and(out_row % rows == row_j, out_row // rows == part_j))

    slot_id = iota((local, HEAD), 0)
    position = jnp.zeros((local, HEAD), F32)
    for l in range(local):
        position = jnp.where(slot_id == l, lengths[l].astype(F32), position)
    angle = position * freq[...]
    cosine = jnp.cos(angle)
    sine = jnp.where(iota((local, HEAD), 1) < HEAD // 2, -1.0, 1.0) * jnp.sin(angle)

    heads_rows = GROUP * local
    a = iota((heads_rows, heads_rows), 0)
    c = iota((heads_rows, heads_rows), 1)
    to_slots = one_hot((a % GROUP) * local + a // GROUP == c)
    head_a = ((a % block) // local) * per + a // block
    to_block = one_hot((a % local) * GROUP + head_a == c)

    def rs_copy(chunk, s):
        half = rows >> (s + 1)
        if s < stages - 1:
            start = (base[s] + (1 - bits[s]) * (n >> (s + 1))) * local
            src = (side if chunk == 0 else queries.at[chunk - 1]).at[pl.ds(pl.multiple_of(start, half), half)]
        else:
            src = side_out if chunk == 0 else query_out.at[chunk - 1]
        dst = side_in[s] if chunk == 0 else query_in[s].at[chunk - 1]
        return pltpu.make_async_remote_copy(
            src_ref=src, dst_ref=dst, send_sem=rs_send.at[chunk, s], recv_sem=rs_recv.at[chunk, s],
            device_id={"wide": partner[s]}, device_id_type=pl.DeviceIdType.MESH)

    def project(chunk):
        arrived(chunk)
        x = gained[...]
        if chunk == 0:
            side[:, :KVCOLS] = dot(x, wk[...])
            side[:, KVCOLS:2 * KVCOLS] = dot(x, wv[...])
        else:
            g = chunk - 1

            @pl.loop(0, QCOLS // 512)
            def _(i):
                at = pl.ds(pl.multiple_of(i * 512, 512), 512)
                queries[g, :, at] = dot(gained[...], wq[g, :, at])
        rs_copy(chunk, 0).start()

    def kept(chunk, s):
        half = rows >> (s + 1)
        buf = side if chunk == 0 else queries.at[chunk - 1]
        at = pl.ds(pl.multiple_of(base[s + 1] * local, half), half)
        return buf, at

    def reduce(chunk, s):
        rs_copy(chunk, s).wait()
        got = side_in[s] if chunk == 0 else query_in[s].at[chunk - 1]
        if s < stages - 2:
            buf, at = kept(chunk, s)
            buf[at, :] = buf[at, :] + got[...]
            rs_copy(chunk, s + 1).start()
            return None
        if s == stages - 2:
            buf, at = kept(chunk, s)
            value = buf[at, :] + got[...]
            low, high = value[:local], value[local:]
            first = bits[stages - 1] == 0
            (side_out if chunk == 0 else query_out.at[chunk - 1])[...] = jnp.where(first, high, low)
            rs_copy(chunk, s + 1).start()
            return jnp.where(first, low, high)
        return got[...]

    def rotate(value, cos, sin):
        return value * cos + pltpu.roll(value, HEAD // 2, 1) * sin

    def finish_side(value):
        scale = lax.rsqrt(value[:, 2 * KVCOLS:] / (width * n) + 1e-5)
        cos = cosine * scale
        sin = sine * scale
        for h in range(GROUP):
            cos_tile[pl.ds(h * local, local), :] = cos
            sin_tile[pl.ds(h * local, local), :] = sin
        for h in range(KV_HEADS):
            at = slice(h * HEAD, (h + 1) * HEAD)
            key = rotate(value[:, at], cos, sin).astype(BF16)
            new = (value[:, KVCOLS + h * HEAD:KVCOLS + (h + 1) * HEAD] * scale).astype(BF16)
            entries[0, :, at] = key
            entries[1, :, at] = new
            fresh[0, :, at] = key.astype(F32)
            fresh[1, :, at] = new.astype(F32)

    def attend(g, value):
        for h in range(GROUP):
            qs[pl.ds(h * local, local), :] = value[:, h * HEAD:(h + 1) * HEAD]
        query = rotate(qs[...], cos_tile[...], sin_tile[...]).astype(BF16)
        query = dot(to_slots, query).astype(BF16)
        at = slice(g * HEAD, (g + 1) * HEAD)
        factor = HEAD ** -0.5
        for l in range(local):
            q = query[l * GROUP:(l + 1) * GROUP]
            scores = lax.dot_general(q, kc[l, :, at], NT, preferred_element_type=F32) * factor
            scores = jnp.where(iota((GROUP, room), 1) < lengths[l], scores, -1e30)
            own = jnp.sum(q.astype(F32) * fresh[0, l:l + 1, at], axis=1, keepdims=True) * factor
            top = jnp.maximum(jnp.max(scores, axis=1, keepdims=True), own)
            weights = jnp.exp(scores - top)
            own_weight = jnp.exp(own - top)
            total = jnp.sum(weights, axis=1, keepdims=True) + own_weight
            mix = dot(weights.astype(BF16), vc[l, :, at])
            mix = mix + own_weight.astype(BF16).astype(F32) * fresh[1, l:l + 1, at]
            hs[pl.ds(l * GROUP, GROUP), :] = (mix / total).astype(BF16)
        mine = dot(to_block, hs[...]).astype(BF16)
        at_rows = pl.ds(pl.multiple_of(base[stages] * block, block), block)
        for p in range(per):
            gathered[g, at_rows, p * HEAD:(p + 1) * HEAD] = mine[p * block:(p + 1) * block]
        ag_copy(g, 0).start()

    def ag_copy(g, u):
        s = stages - 1 - u
        size = block << u
        at = pl.ds(pl.multiple_of(base[s + 1] * block, size), size)
        ref = gathered.at[g, at]
        return pltpu.make_async_remote_copy(
            src_ref=ref, dst_ref=ref, send_sem=ag_send.at[g, u], recv_sem=ag_recv.at[g, u],
            device_id={"wide": partner[s]}, device_id_type=pl.DeviceIdType.MESH)

    def emit(g):
        arrived(KV_HEADS + 2 + g)
        heads = dot(picks[...], gathered[g]).astype(BF16)
        part_cols = QCOLS // parts
        acc = total_out[...] if g else tokens[...].astype(F32)
        for p in range(parts):
            acc = acc + dot(heads[p * rows:(p + 1) * rows],
                            wo[pl.ds(g * QCOLS + p * part_cols, part_cols), :])
        if g < KV_HEADS - 1:
            total_out[...] = acc
        else:
            mixed[...] = acc.astype(BF16)

    pl.semaphore_wait(barrier, stages)
    chunks = KV_HEADS + 1
    held = {}
    for t in range(chunks + 2 * stages):
        if t < chunks:
            project(t)
            if t == 1:
                begin(chunks)
            if t >= 1:
                begin(chunks + t)
        for chunk in range(chunks):
            s = t - 1 - chunk
            if 0 <= s < stages:
                value = reduce(chunk, s)
                if s == stages - 2:
                    held[chunk] = value
                if s == stages - 1:
                    value = held.pop(chunk) + value
                    if chunk == 0:
                        finish_side(value)
                    else:
                        if chunk == 1:
                            arrived(chunks)
                        attend(chunk - 1, value)
            u = t - 1 - stages - chunk
            if chunk and 0 <= u < stages:
                ag_copy(chunk - 1, u).wait()
                if u < stages - 1:
                    ag_copy(chunk - 1, u + 1).start()
                else:
                    emit(chunk - 1)


def body(tokens, norm_gain, w_query, key_weight, value_weight, w_out,
         cache_keys, value_cache_slots, slot_fill_lengths, slot_rows, *, n):
    rows, width = tokens.shape
    local, room, _ = cache_keys.shape
    stages = n.bit_length() - 1
    out_width = w_out.shape[1]
    half = HEAD // 2
    freq = np.float32(500000.0) ** (-(np.float32(2.0) / np.float32(HEAD)) * np.arange(half, dtype=np.float32))
    freq = jnp.asarray(np.concatenate([freq, freq])[None, :].astype(np.float32))
    vmem = pl.BlockSpec(memory_space=pltpu.VMEM)
    anywhere = pl.BlockSpec(memory_space=pl.ANY)
    halves = [rows >> (s + 1) for s in range(stages)]
    chunks = KV_HEADS + 1
    wide_rows = 16 // local * rows
    scratch = [
        pltpu.VMEM((KV_HEADS, width, QCOLS), BF16),
        pltpu.VMEM((width, KVCOLS), BF16),
        pltpu.VMEM((width, KVCOLS), BF16),
        pltpu.VMEM(w_out.shape, BF16),
        pltpu.VMEM(cache_keys.shape, BF16),
        pltpu.VMEM(cache_keys.shape, BF16),
        pltpu.VMEM((rows, width), BF16),
        pltpu.VMEM((rows, SIDE), F32),
        pltpu.VMEM((KV_HEADS, rows, QCOLS), F32),
        *[pltpu.VMEM((h, SIDE), F32) for h in halves],
        *[pltpu.VMEM((KV_HEADS, h, QCOLS), F32) for h in halves],
        pltpu.VMEM((local, SIDE), F32),
        pltpu.VMEM((KV_HEADS, local, QCOLS), F32),
        pltpu.VMEM((KV_HEADS, wide_rows, QCOLS * local // 16), BF16),
        pltpu.VMEM((GROUP * local, HEAD), F32),
        pltpu.VMEM((GROUP * local, HEAD), BF16),
        pltpu.VMEM((GROUP * local, HEAD), F32),
        pltpu.VMEM((GROUP * local, HEAD), F32),
        pltpu.VMEM((2, local, KVCOLS), F32),
        pltpu.VMEM((wide_rows, wide_rows), BF16),
        pltpu.VMEM((rows, out_width), F32),
        pltpu.SemaphoreType.DMA((8 + KV_HEADS,)),
        pltpu.SemaphoreType.DMA((chunks, stages)),
        pltpu.SemaphoreType.DMA((chunks, stages)),
        pltpu.SemaphoreType.DMA((KV_HEADS, stages)),
        pltpu.SemaphoreType.DMA((KV_HEADS, stages)),
    ]
    return pl.pallas_call(
        functools.partial(kernel, n, stages, local, room, width),
        out_shape=(jax.ShapeDtypeStruct((rows, out_width), BF16),
                   jax.ShapeDtypeStruct((2, local, KVCOLS), BF16)),
        in_specs=[pl.BlockSpec(memory_space=pltpu.SMEM)] + [vmem] * 4 + [anywhere] * 6,
        out_specs=(vmem, vmem),
        scratch_shapes=scratch,
        compiler_params=pltpu.CompilerParams(
            collective_id=0, has_side_effects=True, vmem_limit_bytes=60 * 1024 * 1024),
    )(slot_fill_lengths, tokens, norm_gain.reshape(1, width), slot_rows.reshape(1, rows), freq,
      w_query, key_weight, value_weight, w_out, cache_keys, value_cache_slots)


def solution(mesh):
    placed = (
        P("groups", "wide"),
        P("wide"),
        P("wide", None),
        P("wide", None),
        P("wide", None),
        P(None, "wide"),
        P(("groups", "wide"), None, None),
        P(("groups", "wide"), None, None),
        P(("groups", "wide")),
        P("groups"),
    )
    return jax.shard_map(
        functools.partial(body, n=mesh.shape["wide"]),
        mesh=mesh,
        in_specs=placed,
        out_specs=(P("groups", "wide"), P(None, ("groups", "wide"), None)),
        check_vma=False,
    )
```

time: 189 us -> 58.4 us (0.31)
  waiting for transfers between devices: 102 us -> 0 us
  Pallas kernels: 0 us -> 53.4 us
  blocking collectives: 35.2 us -> 0 us
  matrix products: 23.9 us -> 0 us
  between operations: 14.2 us -> 0.64 us
  other arithmetic: 7.3 us -> 0 us
    psum x1 -> x0, waiting for transfers between devices: 66.5 us -> none  [body(): lax.psum((jnp.concatenate([jnp.dot(gained, w_query, preferred_element_typ...]
    pallas_call x0 -> x1, Pallas kernels: none -> 53.4 us  [body(): pl.pallas_call(functools.partial(kernel, n, stages, local, room, width),...]
    all_gather x1 -> x0, waiting for transfers between devices: 35.6 us -> none  [body(): lax.all_gather(heads, 'wide', axis=0, tiled=True)]
    psum x1 -> x0, blocking collectives: 35.2 us -> none  [body(): lax.psum((jnp.concatenate([jnp.dot(gained, w_query, preferred_element_typ...]
    dot_general x7 -> x0, matrix products: 23.9 us -> none  [the longest x1 8.82 us: body(): jnp.dot(lax.all_gather(heads, 'wide', axis=0, tiled=True), w_out, preferr...]
    gather x2 -> x0, local copies, waits for them, and re-layouts: 2.4 us -> none  [the longest x1 1.72 us: body(): ordered = tokens[slot_rows]]
    convert_element_type x7 -> x0, other arithmetic: 2.35 us -> none  [the longest x1 0.81 us: body(): fresh_value = projected_value.astype(jnp.bfloat16)]
  transfers between devices with their start and end apart: 2 -> 0, of which waited for: 2 -> 0; matrix products, arithmetic and copies ran while one was open for 1% -> 0% of each run, Pallas kernels for 0% -> 0%
where the time goes in v1:
time: 58.4 us; the launch traced here: 58.2 us
  Pallas kernels  53.4 us (91%)
  local copies, waits for them, and re-layouts  4.15 us (7%)
  between operations  0.64 us (1%)
    pallas_call x1, Pallas kernels, body(): pl.pallas_call(functools.partial(kernel, n, stages, local, room, width),...  53.4 us
    unnamed x2, local copies, waits for them, and re-layouts  2.87 us
    reshape x1, local copies, waits for them, and re-layouts, body(): norm_gain.reshape(1, width)  1.28 us

profile of v1, /device:TPU:0, one launch (start us, length us, event | category | flops | bytes accessed | tf_op | source)
XLA Modules:
  0.0 58.2 jit_solution(11810990380160705371)
XLA Ops:
  0.6 1.3 %reshape.10.gain = bf16[1,1024]{1,0:T(2,128)(2,1)} reshape(bf16[1024]{0:T(1024)(128)(2,1)} %param.12) | data formatting | bytes 4096 | tf_op jit(solution)/shard_map/reshape | solution.py:327
  1.9 53.4 %shard_map.122 = (bf16[64,1024]{1,0:T(8,128)(2,1)}, bf16[2,4,512]{2,1,0:T(4,128)(2,1)}) custom-call(s32[4]{0:T(128)} %lengths.1, bf16[64,1024]{1,0:T(8,128)(2,1)} %tokens.1, bf16[1,1024]{1,0:T(2,128)(2,1)} %reshape.10.gain, s32[1,64]{1,0:T(1,128)} %bitcast.1, f32[1,128]{1,0:T(1,128)} %constant.2.clone.freq, bf16[1024,8192]{1,0:T(8,128)(2,1)} %wq_hbm.1, ...), custom_call_target="tpu_custom_call" | custom-call | tf_op jit(solution)/shard_map/pallas_call | solution.py:318
  55.3 1.6 %copy.15 = bf16[64,1024]{1,0:T(8,128)(2,1)} copy(bf16[64,1024]{1,0:T(8,128)(2,1)} %get-tuple-element.4) | data formatting | bytes 262144
  56.9 1.3 %copy.16 = bf16[2,4,512]{2,1,0:T(4,128)(2,1)} copy(bf16[2,4,512]{2,1,0:T(4,128)(2,1)} %get-tuple-element.5) | data formatting | bytes 16384
